TPU v7x, 256 devices: a whole 4x4x8 slice. The times are simulated.
256 devices in a mesh: ia: 4 (over z_hi), ja: 16 (over x, z_lo, core), ka: 4 (over y).
Axes of the slice: x: 4, y: 4, z: 8 (z_hi: 4, z_lo: 2; z = z_hi * 2 + z_lo), core: 2. Of those that a mesh axis runs over, the one named last changes fastest.
Arguments:
- tensor: bfloat16 [512, 1024, 1024], P('ia', 'ja', 'ka'), may hold values from -80 to 80
- factor_b: float32 [16, 16, 4, 512], P('ja', ('ia', 'ka')), may hold values from -5 to 5
- factor_c: float32 [4, 64, 4, 512], P('ka', ('ia', 'ja')), may hold values from -5 to 5
Outputs:
- factor_a_new: float32 [4, 64, 2, 512], P('ia', ('ja', 'ka'))
- factor_b_new: float32 [16, 16, 4, 512], P('ja', ('ia', 'ka'))
- factor_c_new: float32 [4, 64, 4, 512], P('ka', ('ia', 'ja'))
All inputs are finite; a program needn't handle non-finite values.
Results may differ from a plain program's by a relative error of at most 0.02.
Values sent between devices are 32-bit elements; how exact they have to be, the bound alone decides.
A program may use at most 128 MiB of HBM per device.

v0:
```python
import jax
import jax.numpy as jnp
from jax import lax
from jax.sharding import PartitionSpec as P

RIDGE = 0.1
EPS = 1e-06


def gram_of(matrix):
    return jnp.dot(
        matrix.T, matrix, precision=lax.Precision.HIGHEST, preferred_element_type=jnp.float32
    )


def solve_rows(partial_value, gram_one, gram_two):
    hadamard = gram_one * gram_two
    ridge = RIDGE * jnp.trace(hadamard) / hadamard.shape[0]
    system = hadamard + ridge * jnp.eye(hadamard.shape[0], dtype=jnp.float32)
    lower = jnp.linalg.cholesky(system)
    middle = lax.linalg.triangular_solve(
        lower, partial_value, left_side=False, lower=True, transpose_a=True
    )
    return lax.linalg.triangular_solve(
        lower, middle, left_side=False, lower=True, transpose_a=False
    )


def rescale_block(raw, gram_raw, count):
    spread = jnp.sqrt(jnp.diagonal(gram_raw) / count + EPS)
    return (raw / spread, gram_raw / (spread[:, None] * spread[None, :]))


def shards(tensor, factor_b, factor_c):
    rank = factor_b.shape[3]
    rows_i, rows_j, rows_k = tensor.shape
    dim_i = rows_i * lax.axis_size("ia")
    dim_j = rows_j * lax.axis_size("ja")
    dim_k = rows_k * lax.axis_size("ka")
    own_rows_a = rows_i // (lax.axis_size("ja") * lax.axis_size("ka"))
    own_rows_b = factor_b.shape[2]
    own_rows_c = factor_c.shape[2]
    block_b = lax.all_gather(factor_b, ("ia", "ka"), axis=1, tiled=True).reshape(rows_j, rank)
    block_c = lax.all_gather(factor_c, ("ia", "ja"), axis=1, tiled=True).reshape(rows_k, rank)
    gram_b = lax.psum(gram_of(block_b), "ja")
    gram_c = lax.psum(gram_of(block_c), "ka")
    half_b = block_b.astype(jnp.bfloat16)
    half_c = block_c.astype(jnp.bfloat16)

    def contract_k(piece):
        return jnp.einsum("ijk,kr->ijr", piece, half_c, preferred_element_type=jnp.float32).astype(
            jnp.bfloat16
        )

    mixed_k = lax.map(contract_k, tensor.reshape(rows_i // 32, 32, rows_j, rows_k)).reshape(
        rows_i, rows_j, rank
    )
    sliced = mixed_k
    part_a = lax.psum_scatter(
        jnp.einsum("ijr,jr->ir", sliced, half_b, preferred_element_type=jnp.float32),
        ("ja", "ka"),
        scatter_dimension=0,
        tiled=True,
    )
    raw_own_a = solve_rows(part_a, gram_b, gram_c)
    raw_a = lax.all_gather(raw_own_a, ("ja", "ka"), axis=0, tiled=True)
    gram_raw_a = lax.psum(gram_of(raw_a), "ia")
    block_a, gram_a = rescale_block(raw_a, gram_raw_a, dim_i)
    new_a = lax.dynamic_slice_in_dim(
        block_a, lax.axis_index(("ja", "ka")) * own_rows_a, own_rows_a, 0
    )
    half_a = block_a.astype(jnp.bfloat16)
    sliced = mixed_k
    part_b = lax.psum_scatter(
        jnp.einsum("ijr,ir->jr", sliced, half_a, preferred_element_type=jnp.float32),
        ("ia", "ka"),
        scatter_dimension=0,
        tiled=True,
    )
    raw_own_b = solve_rows(part_b, gram_a, gram_c)
    raw_b = lax.all_gather(raw_own_b, ("ia", "ka"), axis=0, tiled=True)
    gram_raw_b = lax.psum(gram_of(raw_b), "ja")
    block_b2, gram_b2 = rescale_block(raw_b, gram_raw_b, dim_j)
    new_b = lax.dynamic_slice_in_dim(
        block_b2, lax.axis_index(("ia", "ka")) * own_rows_b, own_rows_b, 0
    )
    half_b2 = block_b2.astype(jnp.bfloat16)

    def mode_three(offset):
        piece = lax.dynamic_slice_in_dim(tensor, offset, 64, 2)
        inner = jnp.einsum("ijk,ir->jkr", piece, half_a, preferred_element_type=jnp.float32).astype(
            jnp.bfloat16
        )
        return jnp.einsum("jkr,jr->kr", inner, half_b2, preferred_element_type=jnp.float32)

    offsets = jnp.arange(rows_k // 64, dtype=jnp.int32) * 64
    local_c = lax.map(mode_three, offsets).reshape(rows_k, rank)
    part_c = lax.psum_scatter(local_c, ("ia", "ja"), scatter_dimension=0, tiled=True)
    raw_own_c = solve_rows(part_c, gram_a, gram_b2)
    raw_c = lax.all_gather(raw_own_c, ("ia", "ja"), axis=0, tiled=True)
    squares_c = lax.psum(jnp.sum(raw_c * raw_c, axis=0), "ka")
    block_c2 = raw_c / jnp.sqrt(squares_c / dim_k + EPS)
    new_c = lax.dynamic_slice_in_dim(
        block_c2, lax.axis_index(("ia", "ja")) * own_rows_c, own_rows_c, 0
    )
    return (
        new_a.reshape(1, 1, own_rows_a, rank),
        new_b.reshape(1, 1, own_rows_b, rank),
        new_c.reshape(1, 1, own_rows_c, rank),
    )


def solution(mesh):
    in_specs = (
        P("ia", "ja", "ka"),
        P("ja", ("ia", "ka"), None, None),
        P("ka", ("ia", "ja"), None, None),
    )
    out_specs = (
        P("ia", ("ja", "ka"), None, None),
        P("ja", ("ia", "ka"), None, None),
        P("ka", ("ia", "ja"), None, None),
    )
    return jax.shard_map(shards, mesh=mesh, in_specs=in_specs, out_specs=out_specs, check_vma=False)
```

profile of v0, /device:TPU:1, one launch (start us, length us, event | category | flops | bytes accessed | tf_op | source)
XLA Modules:
  0.0 1920.0 jit_solution(10290302571989361807)
XLA Ops:
  7.2 41.6 %all_gather.16 = f32[1,16,4,512]{3,2,0,1:T(4,128)S(1)} all-gather(f32[1,1,4,512]{3,2,0,1:T(4,128)} %bitcast.298), channel_id=1, replica_groups=mesh['ia'=4,'ja'=16,'ka'=4] {'ia','ka'}, dimensions={1}, use_global_device_ids=true | all-gather | bytes 139264 | tf_op jit(solution)/shard_map/all_gather | solution.py:43
  48.9 78.9 %all_gather.15 = f32[1,64,4,512]{3,2,0,1:T(4,128)S(1)} all-gather(f32[1,1,4,512]{3,2,0,1:T(4,128)} %bitcast.297), channel_id=1, replica_groups=mesh['ia'=4,'ja'=16,'ka'=4] {'ia','ja'}, dimensions={1}, use_global_device_ids=true | all-gather | bytes 532480 | tf_op jit(solution)/shard_map/all_gather | solution.py:44
  128.0 13.1 while.29
  128.0 3.3 bitcast_dynamic-update-slice_fusion.10
  141.1 6.2 multiply_reduce_fusion.2
  154.3 492.7 %all-reduce.20.cloned.1.call-done = f32[128,512]{0,1:T(8,128)} async-done(((f32[128,512]{0,1:T(8,128)}), f32[128,512]{0,1:T(8,128)}) %all-reduce.20.cloned.1.call-update) | async-done | bytes 262160
  648.3 125.7 %all-reduce.12.cloned.1.call-done = f32[512,512]{0,1:T(8,128)} async-done(((f32[512,512]{0,1:T(8,128)}), f32[512,512]{0,1:T(8,128)}) %all-reduce.12.cloned.1.call-update) | async-done | bytes 1048592 | tf_op jit(solution)/shard_map/psum | solution.py:45
  774.0 52.3 %all-reduce.14.cloned.1.call-done = f32[512,512]{0,1:T(8,128)} async-done(((f32[512,512]{0,1:T(8,128)}), f32[512,512]{0,1:T(8,128)}) %all-reduce.14.cloned.1.call-update) | async-done | bytes 1048592 | tf_op jit(solution)/shard_map/psum | solution.py:46
  830.0 11.7 cholesky.374
  841.9 9.8 custom-call.44
  852.5 11.7 cholesky.393
  864.3 10.0 custom-call.45
  875.4 11.7 cholesky.414
  887.3 9.8 custom-call.46
  897.9 11.9 cholesky.431
  914.8 8.6 while.31
  923.4 39.3 %custom-call.31 = f32[4,128,128]{1,2,0:T(8,128)S(1)} custom-call(f32[4,128,128]{2,1,0:T(8,128)S(1)} %get-tuple-element.85), custom_call_target="InvertDiagBlocksLowerTriangular" | custom-call | tf_op jit(solution)/shard_map/triangular_solve | solution.py:21
  966.6 136.3 %all-gather = f32[64,2,512]{2,1,0:T(2,128)S(1)} all-gather(f32[1,2,512]{2,1,0:T(2,128)S(1)} %maximum_bitcast_fusion.2), channel_id=1, replica_groups=mesh['ia'=4,'ja'=16,'ka'=4] {'ja','ka'}, dimensions={0}, use_global_device_ids=true | all-gather | bytes 266240 | tf_op jit(solution)/shard_map/all_gather | solution.py:66
  1106.4 67.3 %all-reduce.16.cloned.1.call-done = f32[512,512]{0,1:T(8,128)} async-done(((f32[512,512]{0,1:T(8,128)}), f32[512,512]{0,1:T(8,128)}) %all-reduce.16.cloned.1.call-update) | async-done | bytes 1048592 | tf_op jit(solution)/shard_map/psum | solution.py:67
  1173.8 8.6 gather_fusion
  1182.4 5.4 multiply_reduce_fusion.1
  1192.4 11.7 cholesky.446
  1204.3 9.8 custom-call.47
  1216.7 11.7 cholesky.465
  1228.4 10.0 custom-call.48
  1239.9 11.7 cholesky.486
  1251.7 9.8 custom-call.49
  1263.0 12.1 cholesky.503
  1280.4 8.5 while.32
  1288.9 39.3 %custom-call.50 = f32[4,128,128]{1,2,0:T(8,128)S(1)} custom-call(f32[4,128,128]{2,1,0:T(8,128)S(1)} %get-tuple-element.98), custom_call_target="InvertDiagBlocksLowerTriangular" | custom-call | tf_op jit(solution)/shard_map/triangular_solve/custom-call.9 | solution.py:21
  1328.2 13.7 all-reduce.22.cloned.1.call-done
  1347.2 37.3 %all-gather.1 = f32[16,4,512]{2,1,0:T(4,128)S(1)} all-gather(f32[1,4,512]{2,1,0:T(4,128)S(1)} %maximum_bitcast_fusion), channel_id=1, replica_groups=mesh['ia'=4,'ja'=16,'ka'=4] {'ia','ka'}, dimensions={0}, use_global_device_ids=true | all-gather | bytes 139264 | tf_op jit(solution)/shard_map/all_gather | solution.py:81
  1386.6 6.9 copy.67
  1395.4 128.0 %all-reduce.18.cloned.1.call-done = f32[512,512]{0,1:T(8,128)} async-done(((f32[512,512]{0,1:T(8,128)}), f32[512,512]{0,1:T(8,128)}) %all-reduce.18.cloned.1.call-update) | async-done | bytes 1048592 | tf_op jit(solution)/shard_map/psum | solution.py:82
  1523.3 8.6 gather_fusion.1
  1536.5 11.7 cholesky.518
  1548.4 9.8 custom-call.52
  1560.7 11.7 cholesky.537
  1572.5 10.0 custom-call.53
  1584.0 11.7 cholesky.558
  1595.8 9.8 custom-call.54
  1607.0 11.9 cholesky.575
  1621.6 22.0 %while.30 = (s32[]{:T(128)}, f32[4,64,512]{2,1,0:T(8,128)}, s32[4]{0:T(128)S(1)}, bf16[128,64,256]{0,2,1:T(8,128)(2,1)}, bf16[128,512]{1,0:T(8,128)(2,1)S(1)}, /...) while((s32[]{:T(128)}, f32[4,64,512]{2,1,0:T(8,128)}, s32[4]{0:T(128)S(1)}, ...), condition=%wide.region_20.24_spmd, body=%wide.region_19.23_spmd.sunk | while | flops 545259520 | bytes 1900699 | solution.py:97
  1646.3 8.5 while.33
  1654.8 39.3 %custom-call.55 = f32[4,128,128]{1,2,0:T(8,128)S(1)} custom-call(f32[4,128,128]{2,1,0:T(8,128)S(1)} %get-tuple-element.100), custom_call_target="InvertDiagBlocksLowerTriangular" | custom-call | tf_op jit(solution)/shard_map/triangular_solve/custom-call.9 | solution.py:21
  1694.8 129.3 %all-reduce.24.cloned.1.call-done = f32[256,512]{1,0:T(8,128)} async-done(((f32[256,512]{1,0:T(8,128)}), f32[256,512]{1,0:T(8,128)}) %all-reduce.24.cloned.1.call-update) | async-done | bytes 524304
  1829.8 73.8 %all-gather.2 = f32[64,4,512]{2,1,0:T(4,128)S(1)} all-gather(f32[1,4,512]{2,1,0:T(4,128)S(1)} %maximum_bitcast_fusion.1), channel_id=1, replica_groups=mesh['ia'=4,'ja'=16,'ka'=4] {'ia','ja'}, dimensions={0}, use_global_device_ids=true | all-gather | bytes 532480 | tf_op jit(solution)/shard_map/all_gather | solution.py:100
  1903.9 8.5 psum.39
  (256 shorter events, 113.7 us)
Async XLA Ops:
  7.2 639.8 %all-reduce.20.cloned.1.call-start = ((), (), s32[]{:S(2)}) async-start(), calls=%async_computation.4 | async-start | bytes 524288
  141.1 12.0 copy-start.6
  148.2 625.8 %all-reduce.12.cloned.1.call-start = ((), (), s32[]{:S(2)}) async-start(), calls=%async_computation | async-start | bytes 2097152 | tf_op jit(solution)/shard_map/psum | solution.py:45
  150.3 676.0 %all-reduce.14.cloned.1.call-start = ((), (), s32[]{:S(2)}) async-start(), calls=%async_computation.1 | async-start | bytes 2097152 | tf_op jit(solution)/shard_map/psum | solution.py:46
  152.6 1021.2 %all-reduce.16.cloned.1.call-start = ((), (), s32[]{:S(2)}) async-start(), calls=%async_computation.2 | async-start | bytes 2097152 | tf_op jit(solution)/shard_map/psum | solution.py:67
  830.0 275.2 %copy-start.5 = (u32[256]{0:T(256)S(1)}, u32[256]{0:T(256)}, u32[]{:S(2)}) copy-start(u32[256]{0:T(256)} %constant.299) | copy-start | bytes 3076
  965.1 224.0 %copy-start.1 = (f32[512,512]{0,1:T(8,128)S(1)}, f32[512,512]{0,1:T(8,128)}, u32[]{:S(2)}) copy-start(f32[512,512]{0,1:T(8,128)} %all-reduce.14.cloned.1.call-done) | copy-start | bytes 3145732
  1105.1 236.8 %all-reduce.22.cloned.1.call-start = ((), (), s32[]{:S(2)}) async-start(), calls=%async_computation.5 | async-start | bytes 524288
  1173.8 15.4 copy-start
  1188.7 334.6 %all-reduce.18.cloned.1.call-start = ((), (), s32[]{:S(2)}) async-start(), calls=%async_computation.3 | async-start | bytes 2097152 | tf_op jit(solution)/shard_map/psum | solution.py:82
  1191.4 1.0 copy-start.2
  1262.9 130.6 %copy-start.4 = (u32[256]{0:T(256)S(1)}, u32[256]{0:T(256)}, u32[]{:S(2)}) copy-start(u32[256]{0:T(256)} %constant.303) | copy-start | bytes 3076
  1386.6 437.6 %all-reduce.24.cloned.1.call-start = ((), (), s32[]{:S(2)}) async-start(), calls=%async_computation.6 | async-start | bytes 1048576
  1535.5 1.0 copy-start.3
Sparse Core Ops, SparseCore 0:
  148.3 498.6 all-reduce.19
  649.8 124.0 all-reduce.11
  776.3 49.9 all-reduce.13
  1105.2 68.4 all-reduce.15
  1188.8 153.0 all-reduce.21
  1386.7 136.5 all-reduce.17
  1643.7 180.3 all-reduce.23
where the time goes:
time: 1930 us; the launch traced here: 1920 us
  waiting for transfers between devices  1010 us (52%)
  blocking collectives  376 us (19%)
  other arithmetic  375 us (19%)
  local copies, waits for them, and re-layouts  66 us (3%)
  matrix products  58.1 us (3%)
  between operations  26.8 us (1%)
    unnamed x10, waiting for transfers between devices  636 us
    another operation x44, other arithmetic, solve_rows(): lower = jnp.linalg.cholesky(system)  238 us
    all_gather x1, blocking collectives, shards(): raw_a = lax.all_gather(raw_own_a, ('ja', 'ka'), axis=0, tiled=True)  136 us
    psum x1, waiting for transfers between devices, shards(): gram_raw_b = lax.psum(gram_of(raw_b), 'ja')  128 us
    psum x1, waiting for transfers between devices, shards(): gram_b = lax.psum(gram_of(block_b), 'ja')  126 us
    another operation x7, other arithmetic, solve_rows(): lax.linalg.triangular_solve(lower, partial_value, left_side=False, lower=...  118 us
    all_gather x1, blocking collectives, shards(): lax.all_gather(factor_c, ('ia', 'ja'), axis=1, tiled=True)  78.9 us
    all_gather x1, blocking collectives, shards(): raw_c = lax.all_gather(raw_own_c, ('ia', 'ja'), axis=0, tiled=True)  73.8 us
  transfers between devices with their start and end apart: 7, of which 7 were waited for; matrix products, arithmetic and copies ran while one was open for 10% of the time, Pallas kernels for 0%

commit v1 on v0

v1 whole, which is shorter than its diff:
```python
import functools

import jax
import jax.numpy as jnp
from jax import lax
from jax.experimental import pallas as pl
from jax.experimental.pallas import tpu as pltpu
from jax.sharding import PartitionSpec as P

RIDGE = 0.1
EPS = 1e-06
F32 = jnp.float32
BF16 = jnp.bfloat16
RANK = 512
STEPS = 9
EXACT_STEPS = 2


def dot(left, right):
    return jnp.dot(left, right, preferred_element_type=F32)


def dot_rows(left, right):
    return lax.dot_general(left, right, (((0,), (0,)), ((), ())), preferred_element_type=F32)


def split_two(value):
    high = value.astype(BF16)
    low = (value - high.astype(F32)).astype(BF16)
    return high, low


def remote(src, dst, send_sem, recv_sem, device):
    return pltpu.make_async_remote_copy(
        src_ref=src,
        dst_ref=dst,
        send_sem=send_sem,
        recv_sem=recv_sem,
        device_id=device,
        device_id_type=pl.DeviceIdType.MESH,
    )


class Sender:
    def __init__(self, sems):
        self.sems = sems
        self.used = 0
        self.pending = []

    def send(self, src, dst, recv_sem, device, cond=None):
        sem = self.sems.at[self.used]
        self.used += 1
        copy = remote(src, dst, sem, recv_sem, device)
        if cond is None:
            copy.start()
        else:
            pl.when(cond)(copy.start)
        self.pending.append((copy, cond))

    def finish(self):
        for copy, cond in self.pending:
            if cond is None:
                copy.wait_send()
            else:
                pl.when(cond)(copy.wait_send)


def kernel(
    t_hbm, fb_ref, fc_ref, a_out, b_out, c_out,
    t_ref, mixed, own8, sib8, g1, ga, gb,
    pa, pb, pc, ra1, ra2, ra3, ra4, rb1, sb, rb2, rc1, sc, rc2, tc, rc3,
    rq1, rq2, rq3, sq1, sq2, sq3,
    mh, ml, gram_b, gram_c, gram_a, gram_b2, dmat, dh, dl, d3,
    bblk, cblk, ablk, b2blk, pvec,
    send_sems, r_sib, r_p0, r_p1, r_p2, r_p3, r_a, r_b, r_c, r_q, t_sem,
):
    ia = lax.axis_index("ia")
    ja = lax.axis_index("ja")
    ka = lax.axis_index("ka")
    core = lax.rem(ja, 2)
    zlo = lax.rem(ja // 2, 2)
    x = ja // 4
    y = ka
    z = ia * 2 + zlo
    half = ia // 2
    sel0 = 1 - core
    u = x * sel0 + y * core
    v = y * sel0 + x * core

    def dev(px, py, pz, pcore):
        return (pz // 2, px * 4 + lax.rem(pz, 2) * 2 + pcore, py)

    def dev_uv(pu, pv):
        return dev(pu * sel0 + pv * core, pv * sel0 + pu * core, z, core)

    sibling = dev(x, y, z, 1 - core)

    def at_x(d):
        return dev(lax.rem(x + d, 4), y, z, core)

    def at_y(d):
        return dev(x, lax.rem(y + d, 4), z, core)

    def at_z(d):
        return dev(x, y, lax.rem(z + d, 8), core)

    load_t = pltpu.make_async_copy(t_hbm, t_ref, t_sem)
    load_t.start()
    out = Sender(send_sems)

    barrier = pltpu.get_barrier_semaphore()
    partners = [sibling]
    partners += [at_x(d) for d in (1, 2, 3)]
    partners += [at_y(d) for d in (1, 2, 3)]
    partners += [at_z(d) for d in range(1, 8)]
    for partner in partners:
        pl.semaphore_signal(
            barrier, inc=1, device_id=partner, device_id_type=pl.DeviceIdType.MESH
        )

    own8[0:4, :] = fb_ref[0, 0]
    own8[4:8, :] = fc_ref[0, 0]
    pl.semaphore_wait(barrier, len(partners))

    def gather_all(buf, slot, slots, contributes, stage):
        me_contributes = contributes
        for d in range(1, 8):
            out.send(
                buf.at[core, v, u, slot], buf.at[core, v, u, slot],
                r_p0.at[stage, slot], at_z(d), me_contributes,
            )
        for s in range(slots):
            if slots == 4:
                other = jnp.logical_or(core != half, slot != s)
            else:
                other = jnp.logical_not(jnp.logical_and(me_contributes, slot == s))
            copy = remote(
                buf.at[core, v, u, s], buf.at[core, v, u, s], send_sems.at[0],
                r_p0.at[stage, s], at_z(1),
            )
            pl.when(other)(copy.wait_recv)
        for d in (1, 3, 2):
            out.send(
                buf.at[core, v, u], buf.at[core, v, u], r_p1.at[stage, d - 1],
                dev_uv(lax.rem(u + d, 4), v),
            )
        for d in (1, 3, 2):
            copy = remote(
                buf.at[core, v, d], buf.at[core, v, d], send_sems.at[0],
                r_p1.at[stage, d - 1], at_z(1),
            )
            copy.wait_recv()
        for d in (1, 3, 2):
            out.send(
                buf.at[core, v], buf.at[core, v], r_p2.at[stage, d - 1],
                dev_uv(u, lax.rem(v + d, 4)),
            )
        out.send(buf.at[core, v], buf.at[core, v], r_p3.at[stage, 0], sibling)
        for d in (1, 3, 2):
            slab = lax.rem(v + 4 - d, 4)
            copy = remote(
                buf.at[core, slab], buf.at[core, slab], send_sems.at[0],
                r_p2.at[stage, d - 1], at_z(1),
            )
            copy.wait_recv()
            out.send(buf.at[core, slab], buf.at[core, slab], r_p3.at[stage, d], sibling)
        for d in range(4):
            copy = remote(
                buf.at[1 - core, d], buf.at[1 - core, d], send_sems.at[0],
                r_p3.at[stage, d], at_z(1),
            )
            copy.wait_recv()

    def recv(ref, sem):
        return remote(ref, ref, send_sems.at[0], sem, sibling)

    def gram(out_ref, rows):
        def body(n, carry):
            rs = pl.ds(pl.multiple_of(n * 256, 256), 256)
            high, low = mh[rs, :], ml[rs, :]
            out_ref[...] += dot_rows(high, high) + dot_rows(high, low) + dot_rows(low, high)
            return carry

        out_ref[...] = jnp.zeros_like(out_ref)
        lax.fori_loop(0, rows // 256, body, 0)

    def start_chain(one, two):
        def eye(n):
            row = lax.broadcasted_iota(jnp.int32, (64, RANK), 0) + n * 64
            col = lax.broadcasted_iota(jnp.int32, (64, RANK), 1)
            return row == col

        def first(n, carry):
            trace, frob = carry
            rs = pl.ds(pl.multiple_of(n * 64, 64), 64)
            value = one[rs, :] * two[rs, :]
            dmat[rs, :] = value
            trace += jnp.sum(jnp.where(eye(n), value, 0.0), axis=0, keepdims=True)
            frob += jnp.sum(value * value, axis=0, keepdims=True)
            return trace, frob

        zero = jnp.zeros((1, RANK), F32)
        trace, frob = lax.fori_loop(0, 8, first, (zero, zero))
        ridge = RIDGE * jnp.sum(trace, axis=1, keepdims=True) / RANK
        top = ridge + jnp.sqrt(jnp.sum(frob, axis=1, keepdims=True))
        scale = 2.0 / (top + ridge)
        sigma = (top + ridge) / (top - ridge)

        def second(n, carry):
            rs = pl.ds(pl.multiple_of(n * 64, 64), 64)
            value = (dmat[rs, :] + jnp.where(eye(n), ridge, 0.0)) * scale
            dmat[rs, :] = value
            high, low = split_two(value)
            dh[0, rs, :] = high
            dl[0, rs, :] = low
            d3[rs, :] = (value - high.astype(F32) - low.astype(F32)).astype(BF16)
            return carry

        lax.fori_loop(0, 8, second, 0)
        factors = []
        for q in range(STEPS):
            twice = 2.0 * sigma * sigma
            factors.append(twice / (twice - 1.0))
            sigma = twice - 1.0
        return scale, factors

    def chain_step(q, factor):
        def body(n, carry):
            cs = pl.ds(pl.multiple_of(n * 256, 256), 256)
            high, low = dh[q], dl[q]
            square = dot(high, dh[q, :, cs]) + dot(high, dl[q, :, cs]) + dot(low, dh[q, :, cs])
            if q < EXACT_STEPS:
                square += (
                    dot(low, dl[q, :, cs]) + dot(high, d3[:, cs]) + dot(d3[...], dh[q, :, cs])
                )
            value = factor * (2.0 * dmat[:, cs] - square)
            dmat[:, cs] = value
            high, low = split_two(value)
            dh[q + 1, :, cs] = high
            dl[q + 1, :, cs] = low
            return carry

        lax.fori_loop(0, 2, body, 0)
        if q + 1 < EXACT_STEPS:
            def third(n, carry):
                rs = pl.ds(pl.multiple_of(n * 64, 64), 64)
                d3[rs, :] = (
                    dmat[rs, :] - dh[q + 1, rs, :].astype(F32) - dl[q + 1, rs, :].astype(F32)
                ).astype(BF16)
                return carry

            lax.fori_loop(0, 8, third, 0)

    def apply_step(q, factor, value):
        high, low = split_two(value)
        both = jnp.concatenate([high.astype(F32), low.astype(F32)], axis=0).astype(BF16)
        wide = dot(both, dh[q])
        narrow = dot(both, dl[q])
        return factor * (2.0 * value - (wide[0:8] + wide[8:16] + narrow[0:8]))

    def solve(rows, scale, factors):
        value = rows * scale
        for q in range(STEPS):
            value = apply_step(q, factors[q], value)
        return value

    to_sib = remote(own8, sib8, send_sems.at[0], r_sib.at[0], sibling)
    to_sib.start()
    out.used = 1
    out.pending.append((to_sib, None))
    to_sib.wait_recv()
    slot = lax.rem(ia, 2) * 2 + zlo
    contributes = core == half

    @pl.when(jnp.logical_and(contributes, core == 0))
    def _():
        g1[core, v, u, slot, 0:4, :] = own8[0:4, :]
        g1[core, v, u, slot, 4:8, :] = sib8[0:4, :]
        g1[core, v, u, slot, 8:12, :] = own8[4:8, :]
        g1[core, v, u, slot, 12:16, :] = sib8[4:8, :]

    @pl.when(jnp.logical_and(contributes, core == 1))
    def _():
        g1[core, v, u, slot, 0:4, :] = sib8[0:4, :]
        g1[core, v, u, slot, 4:8, :] = own8[0:4, :]
        g1[core, v, u, slot, 8:12, :] = sib8[4:8, :]
        g1[core, v, u, slot, 12:16, :] = own8[4:8, :]

    gather_all(g1, slot, 4, contributes, 0)

    def fill_c(n, carry):
        pia, rest = n // 8, lax.rem(n, 8)
        px, pzlo = rest // 2, lax.rem(rest, 2)
        ph = pia // 2
        pu = px * (1 - ph) + y * ph
        pv = y * (1 - ph) + px * ph
        ps = lax.rem(pia, 2) * 2 + pzlo
        cblk[pl.ds(pl.multiple_of(n * 8, 8), 8), :] = g1[ph, pv, pu, ps, 8:16, :]
        return carry

    lax.fori_loop(0, 32, fill_c, 0)

    def fill_b(n, carry):
        pia, py = n // 2, lax.rem(n, 2) * 2
        ph = pia // 2
        ps = lax.rem(pia, 2) * 2 + zlo

        def piece(yy):
            pu = x * (1 - ph) + yy * ph
            pv = yy * (1 - ph) + x * ph
            return g1[ph, pv, pu, ps, 0:8, :]

        one, two = piece(py), piece(py + 1)

        @pl.when(core == 0)
        def _():
            pvec[0:4, :] = one[0:4]
            pvec[4:8, :] = two[0:4]

        @pl.when(core == 1)
        def _():
            pvec[0:4, :] = one[4:8]
            pvec[4:8, :] = two[4:8]

        bblk[pl.ds(pl.multiple_of(n * 8, 8), 8), :] = pvec[...].astype(BF16).astype(F32)
        return carry

    lax.fori_loop(0, 8, fill_b, 0)

    load_t.wait()

    def contract(g, carry):
        half_c = cblk[...].astype(BF16)
        weight = bblk[...]
        parts = []
        for s in range(2):
            piece = t_ref[pl.ds(g * 8 + s * 4, 4)].reshape(256, 256)
            value = dot(piece, half_c).astype(BF16).reshape(4, 64, RANK)
            mixed[pl.ds(g * 8 + s * 4, 4)] = value
            parts.append(jnp.sum(value.astype(F32) * weight[None], axis=1))
        pa[g] = jnp.concatenate(parts, axis=0)
        return carry

    lax.fori_loop(0, 16, contract, 0)

    not_half = core != half
    out.send(pa, ra1, r_a.at[0], sibling, not_half)

    def load_g1(offset):
        def body(n, carry):
            ph = n // 16
            pv = lax.rem(n // 4, 4)
            pu = lax.rem(n, 4)
            rows = g1[ph, pv, pu, :, offset:offset + 8, :].reshape(32, RANK)
            high, low = split_two(rows)
            rs = pl.ds(pl.multiple_of(n * 32, 32), 32)
            mh[rs, :] = high
            ml[rs, :] = low
            return carry

        lax.fori_loop(0, 32, body, 0)

    load_g1(0)
    gram(gram_b, 1024)
    a_owner = jnp.logical_and(core == half, lax.rem(x, 2) == zlo)

    @pl.when(core == half)
    def _():
        recv(ra1, r_a.at[0]).wait_recv()
        pa[...] += ra1[...]

    for m in range(2):
        px = 1 - zlo + 2 * m
        out.send(
            pa.at[pl.ds(px * 4, 4)], ra2.at[m], r_a.at[1 + m],
            dev(x, y, ia * 2 + 1 - zlo, core), core == half,
        )
    load_g1(8)
    gram(gram_c, 1024)

    @pl.when(core == half)
    def _():
        for m in range(2):
            recv(ra2.at[m], r_a.at[1 + m]).wait_recv()
            px = zlo + 2 * m
            pa[pl.ds(px * 4, 4)] += ra2[m]

    for d in (1, 2, 3):
        px = lax.rem(x + d, 4)
        out.send(
            pa.at[pl.ds(px * 4, 4)], ra3.at[d - 1], r_a.at[2 + d], at_x(d),
            jnp.logical_and(core == half, lax.rem(px, 2) == zlo),
        )
    scale, factors = start_chain(gram_b, gram_c)
    chain_step(0, factors[0])

    @pl.when(a_owner)
    def _():
        for d in (1, 2, 3):
            recv(ra3.at[d - 1], r_a.at[2 + d]).wait_recv()
        pa[pl.ds(x * 4, 4)] += ra3[0] + ra3[1] + ra3[2]

    for d in (1, 2, 3):
        out.send(
            pa.at[x * 4 + lax.rem(y + d, 4)], ra4.at[d - 1], r_a.at[5 + d], at_y(d), a_owner
        )
    for q in range(1, STEPS - 1):
        chain_step(q, factors[q])

    aslot = lax.rem(ia, 2)

    @pl.when(a_owner)
    def _():
        for d in (1, 2, 3):
            recv(ra4.at[d - 1], r_a.at[5 + d]).wait_recv()
        rows = pa[x * 4 + y] + ra4[0] + ra4[1] + ra4[2]
        ga[core, v, u, aslot] = solve(rows, scale, factors)

    gather_all(ga, aslot, 2, a_owner, 1)

    def scale_rows(buf, count, rows):
        def squares(n, total):
            value = buf[n // 16, lax.rem(n // 4, 4), lax.rem(n, 4)].reshape(rows, RANK)
            return total + jnp.sum(value * value, axis=0, keepdims=True)

        total = lax.fori_loop(0, 32, squares, jnp.zeros((1, RANK), F32))
        spread = jnp.sqrt(total / count + EPS)

        def normal(n, carry):
            value = buf[n // 16, lax.rem(n // 4, 4), lax.rem(n, 4)].reshape(rows, RANK) / spread
            high, low = split_two(value)
            rs = pl.ds(pl.multiple_of(n * rows, rows), rows)
            mh[rs, :] = high
            ml[rs, :] = low
            return carry

        lax.fori_loop(0, 32, normal, 0)
        return spread

    spread_a = scale_rows(ga, 512, 16)

    def fill_a(n, carry):
        px, py = n // 4, lax.rem(n, 4)
        pu = px * (1 - half) + py * half
        pv = py * (1 - half) + px * half
        ablk[pl.ds(pl.multiple_of(n * 8, 8), 8), :] = ga[half, pv, pu, aslot] / spread_a
        return carry

    lax.fori_loop(0, 16, fill_a, 0)
    own_a = ablk[pl.ds(pl.multiple_of(ja * 8, 8), 8), :]
    for s in range(4):
        @pl.when(ka == s)
        def _():
            a_out[0, 0] = own_a[2 * s:2 * s + 2]

    def second_mode(g, total):
        rows = ablk[pl.ds(pl.multiple_of(g * 8, 8), 8), :].astype(BF16).astype(F32)
        for s in range(8):
            total = total + mixed[g * 8 + s].astype(F32) * rows[s:s + 1, :]
        return total

    part_b = lax.fori_loop(0, 16, second_mode, jnp.zeros((64, RANK), F32))
    for o in range(8):
        pb[o % 4, o // 4] = part_b[o * 8:o * 8 + 8]
    for d in (1, 2, 3):
        out.send(pb.at[lax.rem(y + d, 4)], rb1.at[d - 1], r_b.at[d - 1], at_y(d))
    gram(gram_a, 512)
    for d in (1, 2, 3):
        recv(rb1.at[d - 1], r_b.at[d - 1]).wait_recv()
    sb[...] = pb[y] + rb1[0] + rb1[1] + rb1[2]
    for d in (1, 2, 3):
        pia = lax.rem(ia + d, 4)
        out.send(
            sb.at[lax.rem(pia, 2)], rb2.at[d - 1], r_b.at[2 + d],
            dev(x, y, pia * 2 + zlo, core), pia // 2 == core,
        )
    scale, factors = start_chain(gram_a, gram_c)
    for q in range(STEPS - 1):
        chain_step(q, factors[q])

    @pl.when(core == half)
    def _():
        for d in (1, 2, 3):
            recv(rb2.at[d - 1], r_b.at[2 + d]).wait_recv()
        rows = sb[lax.rem(ia, 2)] + rb2[0] + rb2[1] + rb2[2]
        gb[core, v, u, slot] = solve(rows, scale, factors)

    gather_all(gb, slot, 4, contributes, 2)
    spread_b = scale_rows(gb, 1024, 32)

    def fill_b2(n, carry):
        py = lax.rem(n, 4)
        pu = x * sel0 + py * core
        pv = py * sel0 + x * core
        b2blk[pl.ds(pl.multiple_of(n * 8, 8), 8), :] = gb[core, pv, pu, (n // 4) * 2 + zlo] / spread_b
        return carry

    lax.fori_loop(0, 8, fill_b2, 0)
    own_b = b2blk[pl.ds(pl.multiple_of((ia * 2 + ka // 2) * 8, 8), 8), :]
    for s in range(2):
        @pl.when(lax.rem(ka, 2) == s)
        def _():
            b_out[0, 0] = own_b[4 * s:4 * s + 4]

    pc[...] = jnp.zeros_like(pc)

    def third_mode(g, carry):
        rows = ablk[pl.ds(pl.multiple_of(g * 8, 8), 8), :].astype(BF16)
        half_b2 = b2blk[...].astype(BF16)
        for s in range(2):
            piece = t_ref[pl.ds(g * 8 + s * 4, 4)].reshape(256, 256)
            weight = jnp.concatenate(
                [half_b2 * rows[s * 4 + n:s * 4 + n + 1, :] for n in range(4)], axis=0
            )
            pc[...] += dot_rows(piece, weight).reshape(4, 4, 2, 8, RANK)
        return carry

    lax.fori_loop(0, 16, third_mode, 0)
    for d in (1, 2, 3):
        out.send(pc.at[:, lax.rem(x + d, 4)], rc1.at[d - 1], r_c.at[d - 1], at_x(d))
    gram(gram_b2, 1024)
    for d in (1, 2, 3):
        recv(rc1.at[d - 1], r_c.at[d - 1]).wait_recv()
    sc[...] = pc[:, x] + rc1[0] + rc1[1] + rc1[2]
    for d in range(1, 8):
        pz = lax.rem(z + d, 8)
        out.send(sc.at[pz // 2, lax.rem(pz, 2)], rc2.at[d - 1], r_c.at[2 + d], at_z(d))
    scale, factors = start_chain(gram_a, gram_b2)
    for q in range(STEPS - 1):
        chain_step(q, factors[q])
        if q == 2:
            for d in range(1, 8):
                recv(rc2.at[d - 1], r_c.at[2 + d]).wait_recv()
            total = sc[ia, zlo]
            for d in range(7):
                total = total + rc2[d]
            tc[...] = total
            out.send(tc, rc3, r_c.at[10], sibling)
    recv(rc3, r_c.at[10]).wait_recv()
    raw = solve(tc[...] + rc3[...], scale, factors)

    sq1[...] = raw * raw
    for d in (1, 2, 3):
        out.send(sq1, rq1.at[d - 1], r_q.at[d - 1], at_x(d))
    for d in (1, 2, 3):
        recv(rq1.at[d - 1], r_q.at[d - 1]).wait_recv()
    sq2[...] = sq1[...] + rq1[0] + rq1[1] + rq1[2]
    for d in (1, 2, 3):
        out.send(sq2, rq2.at[d - 1], r_q.at[2 + d], at_y(d))
    for d in (1, 2, 3):
        recv(rq2.at[d - 1], r_q.at[2 + d]).wait_recv()
    sq3[...] = sq2[...] + rq2[0] + rq2[1] + rq2[2]
    for d in range(1, 8):
        out.send(sq3, rq3.at[d - 1], r_q.at[5 + d], at_z(d))
    for d in range(1, 8):
        recv(rq3.at[d - 1], r_q.at[5 + d]).wait_recv()
    total = sq3[...]
    for d in range(7):
        total = total + rq3[d]
    spread = jnp.sqrt(jnp.sum(total, axis=0, keepdims=True) / 1024 + EPS)
    final = raw / spread
    for s in range(2):
        @pl.when(core == s)
        def _():
            c_out[0, 0] = final[4 * s:4 * s + 4]

    out.finish()


def shards(tensor, factor_b, factor_c):
    vmem = pltpu.VMEM
    dma = pltpu.SemaphoreType.DMA
    scratch = [
        vmem((128, 64, 256), BF16),
        vmem((128, 64, RANK), BF16),
        vmem((8, RANK), F32),
        vmem((8, RANK), F32),
        vmem((2, 4, 4, 4, 16, RANK), F32),
        vmem((2, 4, 4, 2, 8, RANK), F32),
        vmem((2, 4, 4, 4, 8, RANK), F32),
        vmem((16, 8, RANK), F32),
        vmem((4, 2, 8, RANK), F32),
        vmem((4, 4, 2, 8, RANK), F32),
        vmem((16, 8, RANK), F32),
        vmem((2, 4, 8, RANK), F32),
        vmem((3, 4, 8, RANK), F32),
        vmem((3, 8, RANK), F32),
        vmem((3, 2, 8, RANK), F32),
        vmem((2, 8, RANK), F32),
        vmem((3, 8, RANK), F32),
        vmem((3, 4, 2, 8, RANK), F32),
        vmem((4, 2, 8, RANK), F32),
        vmem((7, 8, RANK), F32),
        vmem((8, RANK), F32),
        vmem((8, RANK), F32),
        vmem((3, 8, RANK), F32),
        vmem((3, 8, RANK), F32),
        vmem((7, 8, RANK), F32),
        vmem((8, RANK), F32),
        vmem((8, RANK), F32),
        vmem((8, RANK), F32),
        vmem((1024, RANK), BF16),
        vmem((1024, RANK), BF16),
        vmem((RANK, RANK), F32),
        vmem((RANK, RANK), F32),
        vmem((RANK, RANK), F32),
        vmem((RANK, RANK), F32),
        vmem((RANK, RANK), F32),
        vmem((STEPS, RANK, RANK), BF16),
        vmem((STEPS, RANK, RANK), BF16),
        vmem((RANK, RANK), BF16),
        vmem((64, RANK), F32),
        vmem((256, RANK), F32),
        vmem((128, RANK), F32),
        vmem((64, RANK), F32),
        vmem((8, RANK), F32),
        dma((112,)),
        dma((1,)),
        dma((3, 4)),
        dma((3, 3)),
        dma((3, 3)),
        dma((3, 4)),
        dma((9,)),
        dma((6,)),
        dma((11,)),
        dma((13,)),
        dma,
    ]
    return pl.pallas_call(
        kernel,
        out_shape=(
            jax.ShapeDtypeStruct((1, 1, 2, RANK), F32),
            jax.ShapeDtypeStruct((1, 1, 4, RANK), F32),
            jax.ShapeDtypeStruct((1, 1, 4, RANK), F32),
        ),
        in_specs=[
            pl.BlockSpec(memory_space=pl.ANY),
            pl.BlockSpec(memory_space=pltpu.VMEM),
            pl.BlockSpec(memory_space=pltpu.VMEM),
        ],
        out_specs=[pl.BlockSpec(memory_space=pltpu.VMEM)] * 3,
        scratch_shapes=scratch,
        compiler_params=pltpu.CompilerParams(
            collective_id=0, has_side_effects=True, vmem_limit_bytes=58 * 1024 * 1024
        ),
        name="sweep",
    )(tensor, factor_b, factor_c)


def solution(mesh):
    in_specs = (
        P("ia", "ja", "ka"),
        P("ja", ("ia", "ka"), None, None),
        P("ka", ("ia", "ja"), None, None),
    )
    out_specs = (
        P("ia", ("ja", "ka"), None, None),
        P("ja", ("ia", "ka"), None, None),
        P("ka", ("ia", "ja"), None, None),
    )
    return jax.shard_map(shards, mesh=mesh, in_specs=in_specs, out_specs=out_specs, check_vma=False)
```

time: 1930 us -> 175 us (0.09)
  waiting for transfers between devices: 1010 us -> 0 us
  blocking collectives: 376 us -> 0 us
  other arithmetic: 375 us -> 0 us
  Pallas kernels: 0 us -> 171 us
  local copies, waits for them, and re-layouts: 66 us -> 3.86 us
  matrix products: 58.1 us -> 0 us
  between operations: 26.8 us -> 0.64 us
    unnamed x10 -> x0, waiting for transfers between devices: 636 us -> none
    psum x4 -> x0, waiting for transfers between devices: 373 us -> none  [the longest x1 128 us: shards(): gram_raw_b = lax.psum(gram_of(raw_b), 'ja')]
    all_gather x5 -> x0, blocking collectives: 368 us -> none  [the longest x1 136 us: shards(): raw_a = lax.all_gather(raw_own_a, ('ja', 'ka'), axis=0, tiled=True)]
    another operation x51 -> x0, other arithmetic: 356 us -> none  [the longest x44 238 us: solve_rows(): lower = jnp.linalg.cholesky(system)]
    pallas_call x0 -> x1, Pallas kernels: none -> 171 us  [shards(): pl.pallas_call(kernel, out_shape=(jax.ShapeDtypeStruct((1, 1, 2, RANK), F...]
    dot_general x12 -> x0, matrix products: 31.4 us -> none  [the longest x4 13 us: contract_k(): jnp.einsum('ijk,kr->ijr', piece, half_c, preferred_element_type=jnp.float32)]
    another operation x68 -> x0, local copies, waits for them, and re-layouts: 28.3 us -> none  [the longest x27 18.9 us: solve_rows(): lax.linalg.triangular_solve(lower, partial_value, left_side=False, lower=...]
    another operation x60 -> x0, matrix products: 26.7 us -> none  [the longest x18 13.3 us: solve_rows(): lower = jnp.linalg.cholesky(system)]
  transfers between devices with their start and end apart: 7 -> 0, of which waited for: 7 -> 0; matrix products, arithmetic and copies ran while one was open for 10% -> 0% of each run, Pallas kernels for 0% -> 0%
where the time goes in v1:
time: 175 us
  Pallas kernels  171 us (98%)
  local copies, waits for them, and re-layouts  3.86 us (2%)
    pallas_call x1, Pallas kernels, shards(): pl.pallas_call(kernel, out_shape=(jax.ShapeDtypeStruct((1, 1, 2, RANK), F...  171 us
    unnamed x3, local copies, waits for them, and re-layouts  3.86 us

profile of v1, /device:TPU:1, one launch (start us, length us, event | category | flops | bytes accessed | tf_op | source)
XLA Modules:
  0.0 175.1 jit_solution(7431367891890898487)
XLA Ops:
  0.6 170.6 %sweep.1 = (f32[1,1,2,512]{3,2,1,0:T(2,128)}, f32[1,1,4,512]{3,2,1,0:T(4,128)}, f32[1,1,4,512]{3,2,1,0:T(4,128)}) custom-call(bf16[128,64,256]{2,1,0:T(8,128)(2,1)} %t_hbm.1, f32[1,1,4,512]{3,2,1,0:T(4,128)} %fb_ref.1, f32[1,1,4,512]{3,2,1,0:T(4,128)} %fc_ref.1), custom_call_target="tpu_custom_call" | custom-call | tf_op jit(solution)/shard_map/sweep/pallas_call | solution.py:629
  171.2 1.3 copy.9
  172.5 1.3 copy.10
  173.8 1.3 copy.11

commit v2 on v1

v2 whole, which is shorter than its diff:
```python
import functools

import jax
import jax.numpy as jnp
from jax import lax
from jax.experimental import pallas as pl
from jax.experimental.pallas import tpu as pltpu
from jax.sharding import PartitionSpec as P

RIDGE = 0.1
EPS = 1e-06
F32 = jnp.float32
BF16 = jnp.bfloat16
RANK = 512
STEPS = 9
EXACT_STEPS = 1


def dot(left, right):
    return jnp.dot(left, right, preferred_element_type=F32)


def dot_rows(left, right):
    return lax.dot_general(left, right, (((0,), (0,)), ((), ())), preferred_element_type=F32)


def split_two(value):
    high = value.astype(BF16)
    low = (value - high.astype(F32)).astype(BF16)
    return high, low


def remote(src, dst, send_sem, recv_sem, device):
    return pltpu.make_async_remote_copy(
        src_ref=src,
        dst_ref=dst,
        send_sem=send_sem,
        recv_sem=recv_sem,
        device_id=device,
        device_id_type=pl.DeviceIdType.MESH,
    )


class Sender:
    def __init__(self, sems):
        self.sems = sems
        self.used = 0
        self.pending = []

    def send(self, src, dst, recv_sem, device, cond=None):
        sem = self.sems.at[self.used]
        self.used += 1
        copy = remote(src, dst, sem, recv_sem, device)
        if cond is None:
            copy.start()
        else:
            pl.when(cond)(copy.start)
        self.pending.append((copy, cond))

    def finish(self):
        for copy, cond in self.pending:
            if cond is None:
                copy.wait_send()
            else:
                pl.when(cond)(copy.wait_send)


def kernel(
    t_hbm, fb_ref, fc_ref, a_out, b_out, c_out,
    t_ref, tt, mixed, arep, own8, sib8, g_b, g_c, ga, gb,
    pa, pb, pc, ra1, ra2, ra3, ra4, rb1, sb, rb2, rc0, rc1, sc, rc2, tc, rc3,
    rq1, rq2, rq3, sq1, sq2, sq3,
    mh, ml, gram_b, gram_c, gram_a, gram_b2, dmat, dh, dl, d3, yvec,
    bblk, cblk, ablk, b2blk, pvec,
    send_sems, r_sib, r_p0, r_p1, r_p2, r_p3, r_a, r_b, r_c, r_q, t_sem,
):
    ia = lax.axis_index("ia")
    ja = lax.axis_index("ja")
    ka = lax.axis_index("ka")
    core = lax.rem(ja, 2)
    zlo = lax.rem(ja // 2, 2)
    x = ja // 4
    y = ka
    z = ia * 2 + zlo
    half = ia // 2
    sel0 = 1 - core

    def dev(px, py, pz, pcore):
        return (pz // 2, px * 4 + lax.rem(pz, 2) * 2 + pcore, py)

    sibling = dev(x, y, z, 1 - core)

    def at_x(d):
        return dev(lax.rem(x + d, 4), y, z, core)

    def at_y(d):
        return dev(x, lax.rem(y + d, 4), z, core)

    def at_z(d):
        return dev(x, y, lax.rem(z + d, 8), core)

    load_t = pltpu.make_async_copy(t_hbm, t_ref, t_sem)
    load_t.start()
    out = Sender(send_sems)

    barrier = pltpu.get_barrier_semaphore()
    partners = [sibling]
    partners += [at_x(d) for d in (1, 2, 3)]
    partners += [at_y(d) for d in (1, 2, 3)]
    partners += [at_z(d) for d in range(1, 8)]
    for partner in partners:
        pl.semaphore_signal(
            barrier, inc=1, device_id=partner, device_id_type=pl.DeviceIdType.MESH
        )

    own8[0:4, :] = fb_ref[0, 0]
    own8[4:8, :] = fc_ref[0, 0]
    pl.semaphore_wait(barrier, len(partners))

    def recv(ref, sem):
        return remote(ref, ref, send_sems.at[0], sem, sibling)

    class Gather:
        def __init__(self, buf, stage, slots, slot, contributes, u_is_x):
            self.buf, self.stage, self.slots, self.slot = buf, stage, slots, slot
            self.contributes = contributes
            self.u_is_x = u_is_x
            self.u = x * u_is_x + y * (1 - u_is_x)
            self.v = y * u_is_x + x * (1 - u_is_x)
            self.p0 = [r_p0.at[stage, n] for n in range(slots)]
            self.p1 = [r_p1.at[stage, n] for n in range(4)]
            self.p2 = [r_p2.at[stage, n] for n in range(6)]
            self.p3 = [r_p3.at[stage, n] for n in range(4)]

        def near(self, du, dv):
            pu, pv = lax.rem(self.u + du + 4, 4), lax.rem(self.v + dv + 4, 4)
            keep = self.u_is_x
            return dev(pu * keep + pv * (1 - keep), pv * keep + pu * (1 - keep), z, core)

        def move(self, ref, sem, device):
            out.send(ref, ref, sem, device)

        def chunk(self, du, first=None):
            pu = lax.rem(self.u + du + 4, 4)
            if first is None:
                return self.buf.at[core, self.v, pu]
            size = self.slots // 2
            return self.buf.at[core, self.v, pu, pl.ds(first * size, size)]

        def slab(self, dv, first=None):
            pv = lax.rem(self.v + dv + 4, 4)
            if first is None:
                return self.buf.at[core, pv]
            return self.buf.at[core, pv, pl.ds(first * 2, 2)]

        def p0_send(self):
            ref = self.buf.at[core, self.v, self.u, self.slot]
            for d in (4, 3, 5, 2, 6, 1, 7):
                out.send(ref, ref, r_p0.at[self.stage, self.slot], at_z(d), self.contributes)

        def p0_wait(self):
            for s in range(self.slots):
                other = jnp.logical_not(jnp.logical_and(self.contributes, self.slot == s))
                copy = recv(self.buf.at[core, self.v, self.u, s], self.p0[s])
                pl.when(other)(copy.wait_recv)

        def p1_send(self):
            self.move(self.chunk(0), self.p1[0], self.near(1, 0))
            self.move(self.chunk(0), self.p1[1], self.near(-1, 0))

        def p1_forward(self):
            recv(self.chunk(-1), self.p1[0]).wait_recv()
            self.move(self.chunk(-1, 0), self.p1[2], self.near(1, 0))
            recv(self.chunk(1), self.p1[1]).wait_recv()
            self.move(self.chunk(1, 1), self.p1[3], self.near(-1, 0))

        def p1_finish(self):
            recv(self.chunk(-2, 0), self.p1[2]).wait_recv()
            recv(self.chunk(2, 1), self.p1[3]).wait_recv()

        def p2_send(self):
            self.move(self.slab(0, 0), self.p2[0], self.near(0, 1))
            self.move(self.slab(0, 1), self.p2[2], self.near(0, -1))
            self.move(self.slab(0, 1), self.p2[1], self.near(0, 1))
            self.move(self.slab(0, 0), self.p2[3], self.near(0, -1))

        def p3_send(self, dv, n):
            self.move(self.slab(dv), self.p3[n], sibling)

        def p2_forward(self):
            recv(self.slab(-1, 0), self.p2[0]).wait_recv()
            self.move(self.slab(-1, 0), self.p2[4], self.near(0, 1))
            recv(self.slab(1, 1), self.p2[2]).wait_recv()
            self.move(self.slab(1, 1), self.p2[5], self.near(0, -1))

        def p2_mid(self):
            recv(self.slab(-1, 1), self.p2[1]).wait_recv()
            self.p3_send(-1, 1)
            recv(self.slab(1, 0), self.p2[3]).wait_recv()
            self.p3_send(1, 2)

        def p2_finish(self):
            recv(self.slab(2, 0), self.p2[4]).wait_recv()
            recv(self.slab(2, 1), self.p2[5]).wait_recv()
            self.p3_send(2, 3)

        def p3_wait(self, n):
            recv(self.buf.at[1 - core, n], self.p3[n]).wait_recv()

        def rows(self, n):
            step = (0, -1, 1, 2)[n]
            other = self.v if self.stage < 2 else self.u
            mine = self.buf[core, lax.rem(self.v + step + 4, 4)]
            theirs = self.buf[1 - core, lax.rem(other + step + 4, 4)]
            count = 4 * self.slots * 8
            return [mine.reshape(count, RANK), theirs.reshape(count, RANK)]

    def add_gram(out_ref, parts, first):
        size = parts[0].shape[0]
        for n, part in enumerate(parts):
            high, low = split_two(part)
            mh[n * size:(n + 1) * size, :] = high
            ml[n * size:(n + 1) * size, :] = low
        high, low = mh[...], ml[...]
        value = dot_rows(high, high) + dot_rows(high, low) + dot_rows(low, high)
        out_ref[...] = value if first else out_ref[...] + value

    def diagonal(n, value):
        row = lax.broadcasted_iota(jnp.int32, (64, RANK), 0) + n * 64
        col = lax.broadcasted_iota(jnp.int32, (64, RANK), 1)
        return jnp.where(row == col, value, 0.0)

    def normal_gram(ref, count):
        def squares(n, total):
            rs = pl.ds(pl.multiple_of(n * 64, 64), 64)
            return total + jnp.sum(diagonal(n, ref[rs, :]), axis=0, keepdims=True)

        total = lax.fori_loop(0, 8, squares, jnp.zeros((1, RANK), F32))
        inverse = 1.0 / jnp.sqrt(total / count + EPS)

        def body(n, carry):
            rs = pl.ds(pl.multiple_of(n * 64, 64), 64)
            value = ref[rs, :]
            mine = jnp.sum(diagonal(n, value), axis=1, keepdims=True)
            ref[rs, :] = value * (1.0 / jnp.sqrt(mine / count + EPS)) * inverse
            return carry

        lax.fori_loop(0, 8, body, 0)
        return inverse

    def start_chain(one, two):
        def first(n, carry):
            trace, frob = carry
            rs = pl.ds(pl.multiple_of(n * 64, 64), 64)
            value = one[rs, :] * two[rs, :]
            dmat[rs, :] = value
            trace += jnp.sum(diagonal(n, value), axis=0, keepdims=True)
            frob += jnp.sum(value * value, axis=0, keepdims=True)
            return trace, frob

        zero = jnp.zeros((1, RANK), F32)
        trace, frob = lax.fori_loop(0, 8, first, (zero, zero))
        ridge = RIDGE * jnp.sum(trace, axis=1, keepdims=True) / RANK
        top = ridge + jnp.sqrt(jnp.sum(frob, axis=1, keepdims=True))
        scale = 2.0 / (top + ridge)
        sigma = (top + ridge) / (top - ridge)

        def second(n, carry):
            rs = pl.ds(pl.multiple_of(n * 64, 64), 64)
            value = (dmat[rs, :] + diagonal(n, ridge)) * scale
            dmat[rs, :] = value
            high, low = split_two(value)
            dh[0, rs, :] = high
            dl[0, rs, :] = low
            d3[rs, :] = (value - high.astype(F32) - low.astype(F32)).astype(BF16)
            return carry

        lax.fori_loop(0, 8, second, 0)
        factors = []
        for q in range(STEPS):
            twice = 2.0 * sigma * sigma
            factors.append(twice / (twice - 1.0))
            sigma = twice - 1.0
        return scale, factors

    def set_rows(q, value):
        yvec[...] = value
        high, low = split_two(value)
        dh[q, 512:528, :] = jnp.concatenate(
            [high.astype(F32), low.astype(F32)], axis=0
        ).astype(BF16)

    def chain_step(q, factor, with_rows):
        tall = 528 if with_rows else 512
        for n in range(2):
            cs = slice(n * 256, n * 256 + 256)
            high, low = dh[q, 0:tall, :], dl[q]
            right_high, right_low = dh[q, 0:512, cs], dl[q, :, cs]
            one = dot(high, right_high)
            two = dot(high, right_low)
            square = one[0:512] + two[0:512] + dot(low, right_high)
            if q < EXACT_STEPS:
                square += (
                    dot(low, right_low)
                    + dot(dh[q, 0:512, :], d3[:, cs])
                    + dot(d3[...], right_high)
                )
            value = factor * (2.0 * dmat[:, cs] - square)
            dmat[:, cs] = value
            high, low = split_two(value)
            dh[q + 1, 0:512, cs] = high
            dl[q + 1, :, cs] = low
            if with_rows:
                value = one[512:520] + one[520:528] + two[512:520]
                value = factor * (2.0 * yvec[:, cs] - value)
                yvec[:, cs] = value
                high, low = split_two(value)
                dh[q + 1, 512:528, cs] = jnp.concatenate(
                    [high.astype(F32), low.astype(F32)], axis=0
                ).astype(BF16)

    def apply_step(q, factor, value):
        high, low = split_two(value)
        both = jnp.concatenate([high.astype(F32), low.astype(F32)], axis=0).astype(BF16)
        wide = dot(both, dh[q, 0:512, :])
        narrow = dot(both, dl[q])
        return factor * (2.0 * value - (wide[0:8] + wide[8:16] + narrow[0:8]))

    def join(q, rows, scale, factors):
        value = rows * scale
        for n in range(q):
            value = apply_step(n, factors[n], value)
        set_rows(q, value)

    def last_step(factors):
        return apply_step(STEPS - 1, factors[STEPS - 1], yvec[...])

    yvec[...] = jnp.zeros_like(yvec)
    to_sib = remote(own8, sib8, send_sems.at[0], r_sib.at[0], sibling)
    to_sib.start()
    out.used = 1
    out.pending.append((to_sib, None))
    to_sib.wait_recv()
    slot = lax.rem(ia, 2) * 2 + zlo
    contributes = core == half
    all_b = Gather(g_b, 0, 4, slot, contributes, 0)
    all_c = Gather(g_c, 1, 4, slot, contributes, 1)

    for c in range(2):
        @pl.when(jnp.logical_and(contributes, core == c))
        def _():
            for gather, at in ((all_b, 0), (all_c, 4)):
                mine = own8[at:at + 4, :]
                theirs = sib8[at:at + 4, :]
                first, second = (mine, theirs) if c == 0 else (theirs, mine)
                gather.buf[core, gather.v, gather.u, slot, 0:4, :] = first
                gather.buf[core, gather.v, gather.u, slot, 4:8, :] = second

    both = (all_b, all_c)
    for gather in both:
        gather.p0_send()
    for gather in both:
        gather.p0_wait()
        gather.p1_send()
    for gather in both:
        gather.p1_forward()
    for gather in both:
        gather.p1_finish()
        gather.p2_send()
        gather.p3_send(0, 0)

    def fill_c(n, carry):
        pia, rest = n // 8, lax.rem(n, 8)
        px, pzlo = rest // 2, lax.rem(rest, 2)
        ps = lax.rem(pia, 2) * 2 + pzlo
        cblk[pl.ds(pl.multiple_of(n * 8, 8), 8), :] = g_c[pia // 2, y, px, ps]
        return carry

    def fill_b(n, carry):
        pia, py = n // 2, lax.rem(n, 2) * 2
        ps = lax.rem(pia, 2) * 2 + zlo
        one, two = g_b[pia // 2, x, py, ps], g_b[pia // 2, x, py + 1, ps]

        @pl.when(core == 0)
        def _():
            pvec[0:4, :] = one[0:4]
            pvec[4:8, :] = two[0:4]

        @pl.when(core == 1)
        def _():
            pvec[0:4, :] = one[4:8]
            pvec[4:8, :] = two[4:8]

        bblk[pl.ds(pl.multiple_of(n * 8, 8), 8), :] = pvec[...].astype(BF16).astype(F32)
        return carry

    for gather in both:
        gather.p3_wait(0)
    lax.fori_loop(0, 32, fill_c, 0)
    lax.fori_loop(0, 8, fill_b, 0)
    add_gram(gram_b, all_b.rows(0), True)
    for gather in both:
        gather.p2_forward()

    load_t.wait()

    def contract(g, carry):
        half_c = cblk[...].astype(BF16)
        weight = bblk[...]
        parts = []
        for s in range(2):
            piece = t_ref[pl.ds(g * 8 + s * 4, 4)].reshape(256, 256)
            value = dot(piece, half_c).reshape(4, 64, RANK)
            mixed[pl.ds(g * 8 + s * 4, 4)] = value.astype(BF16)
            parts.append(jnp.sum(value * weight[None], axis=1))
        pa[g] = jnp.concatenate(parts, axis=0)
        return carry

    lax.fori_loop(0, 8, contract, 0)
    for gather in both:
        gather.p2_mid()
    lax.fori_loop(8, 16, contract, 0)

    out.send(pa, ra1, r_a.at[0], sibling, core != half)
    for gather in both:
        gather.p2_finish()
    add_gram(gram_c, all_c.rows(0), True)
    for n in (1, 2):
        all_b.p3_wait(n)
        add_gram(gram_b, all_b.rows(n), False)
    a_owner = jnp.logical_and(core == half, lax.rem(x, 2) == zlo)

    @pl.when(core == half)
    def _():
        recv(ra1, r_a.at[0]).wait_recv()
        pa[...] += ra1[...]

    for m in range(2):
        px = 1 - zlo + 2 * m
        out.send(
            pa.at[pl.ds(px * 4, 4)], ra2.at[m], r_a.at[1 + m],
            dev(x, y, ia * 2 + 1 - zlo, core), core == half,
        )
    for n in (1, 2):
        all_c.p3_wait(n)
        add_gram(gram_c, all_c.rows(n), False)

    @pl.when(core == half)
    def _():
        for m in range(2):
            recv(ra2.at[m], r_a.at[1 + m]).wait_recv()
            px = zlo + 2 * m
            pa[pl.ds(px * 4, 4)] += ra2[m]

    for d in (1, 2, 3):
        px = lax.rem(x + d, 4)
        out.send(
            pa.at[pl.ds(px * 4, 4)], ra3.at[d - 1], r_a.at[2 + d], at_x(d),
            jnp.logical_and(core == half, lax.rem(px, 2) == zlo),
        )
    all_b.p3_wait(3)
    add_gram(gram_b, all_b.rows(3), False)
    all_c.p3_wait(3)
    add_gram(gram_c, all_c.rows(3), False)

    @pl.when(a_owner)
    def _():
        for d in (1, 2, 3):
            recv(ra3.at[d - 1], r_a.at[2 + d]).wait_recv()
        pa[pl.ds(x * 4, 4)] += ra3[0] + ra3[1] + ra3[2]

    for d in (1, 2, 3):
        out.send(
            pa.at[x * 4 + lax.rem(y + d, 4)], ra4.at[d - 1], r_a.at[5 + d], at_y(d), a_owner
        )
    scale, factors = start_chain(gram_b, gram_c)
    chain_step(0, factors[0], False)

    @pl.when(a_owner)
    def _():
        for d in (1, 2, 3):
            recv(ra4.at[d - 1], r_a.at[5 + d]).wait_recv()
        rows = pa[x * 4 + y] + ra4[0] + ra4[1] + ra4[2]
        join(1, rows, scale, factors)

    for q in range(1, STEPS - 1):
        chain_step(q, factors[q], True)
    aslot = lax.rem(ia, 2)
    all_a = Gather(ga, 2, 2, aslot, a_owner, sel0)

    @pl.when(a_owner)
    def _():
        ga[core, all_a.v, all_a.u, aslot] = last_step(factors)

    def turn(g, carry):
        tt[g] = t_ref[pl.ds(g * 16, 16)].reshape(1024, 256).T
        return carry

    all_a.p0_send()
    lax.fori_loop(0, 4, turn, 0)
    all_a.p0_wait()
    all_a.p1_send()
    lax.fori_loop(4, 6, turn, 0)
    all_a.p1_forward()
    all_a.p1_finish()
    all_a.p2_send()
    all_a.p3_send(0, 0)
    lax.fori_loop(6, 8, turn, 0)
    all_a.p2_forward()
    all_a.p2_mid()
    all_a.p2_finish()
    all_a.p3_wait(0)
    all_a.p3_wait(1)
    add_gram(gram_a, all_a.rows(0) + all_a.rows(1), True)
    all_a.p3_wait(2)
    all_a.p3_wait(3)
    add_gram(gram_a, all_a.rows(2) + all_a.rows(3), False)
    inverse_a = normal_gram(gram_a, 512)

    def fill_a(n, carry):
        px, py = n // 4, lax.rem(n, 4)
        pu = px * (1 - half) + py * half
        pv = py * (1 - half) + px * half
        ablk[pl.ds(pl.multiple_of(n * 8, 8), 8), :] = ga[half, pv, pu, aslot] * inverse_a
        return carry

    lax.fori_loop(0, 16, fill_a, 0)

    def second_mode(g, total):
        rows = ablk[pl.ds(pl.multiple_of(g * 8, 8), 8), :].astype(BF16).astype(F32)
        for s in range(8):
            total = total + mixed[g * 8 + s].astype(F32) * rows[s:s + 1, :]
        return total

    part_b = lax.fori_loop(0, 16, second_mode, jnp.zeros((64, RANK), F32))
    for o in range(8):
        pb[o % 4, o // 4] = part_b[o * 8:o * 8 + 8]
    for d in (1, 2, 3):
        out.send(pb.at[lax.rem(y + d, 4)], rb1.at[d - 1], r_b.at[d - 1], at_y(d))
    scale, factors = start_chain(gram_a, gram_c)
    chain_step(0, factors[0], False)
    for d in (1, 2, 3):
        recv(rb1.at[d - 1], r_b.at[d - 1]).wait_recv()
    sb[...] = pb[y] + rb1[0] + rb1[1] + rb1[2]
    for d in (1, 2, 3):
        pia = lax.rem(ia + d, 4)
        out.send(
            sb.at[lax.rem(pia, 2)], rb2.at[d - 1], r_b.at[2 + d],
            dev(x, y, pia * 2 + zlo, core), pia // 2 == core,
        )
    own_a = ablk[pl.ds(pl.multiple_of(ja * 8, 8), 8), :]
    for s in range(4):
        @pl.when(ka == s)
        def _():
            a_out[0, 0] = own_a[2 * s:2 * s + 2]

    for q in (1, 2):
        chain_step(q, factors[q], False)

    @pl.when(core == half)
    def _():
        for d in (1, 2, 3):
            recv(rb2.at[d - 1], r_b.at[2 + d]).wait_recv()
        join(3, sb[lax.rem(ia, 2)] + rb2[0] + rb2[1] + rb2[2], scale, factors)

    for q in range(3, STEPS - 1):
        chain_step(q, factors[q], True)
    all_b2 = Gather(gb, 3, 4, slot, contributes, sel0)

    @pl.when(core == half)
    def _():
        gb[core, all_b2.v, all_b2.u, slot] = last_step(factors)

    def repeat_a(g, carry):
        rows = ablk[pl.ds(pl.multiple_of(g * 8, 8), 8), :].astype(BF16).astype(F32)
        for s in range(8):
            arep[g * 8 + s] = jnp.broadcast_to(rows[s:s + 1, :], (16, RANK)).astype(BF16)
        return carry

    all_b2.p0_send()
    lax.fori_loop(0, 16, repeat_a, 0)
    all_b2.p0_wait()
    all_b2.p1_send()
    all_b2.p1_forward()
    all_b2.p1_finish()
    all_b2.p2_send()
    all_b2.p3_send(0, 0)
    all_b2.p2_forward()
    all_b2.p3_wait(0)
    add_gram(gram_b2, all_b2.rows(0), True)
    all_b2.p2_mid()
    all_b2.p2_finish()
    for n in (1, 2, 3):
        all_b2.p3_wait(n)
        add_gram(gram_b2, all_b2.rows(n), False)
    inverse_b = normal_gram(gram_b2, 1024)

    def fill_b2(n, carry):
        py = lax.rem(n, 4)
        pu = x * sel0 + py * core
        pv = py * sel0 + x * core
        rows = gb[core, pv, pu, (n // 4) * 2 + zlo] * inverse_b
        b2blk[pl.ds(pl.multiple_of(n * 8, 8), 8), :] = rows
        return carry

    lax.fori_loop(0, 8, fill_b2, 0)

    pc[...] = jnp.zeros_like(pc)

    def third_mode(g, carry):
        half_b2 = b2blk[...].astype(BF16).reshape(4, 16, RANK)
        weight = jnp.concatenate(
            [(half_b2 * arep[g * 16 + n][None]).reshape(64, RANK) for n in range(16)], axis=0
        )
        pc[...] += dot(tt[g], weight).reshape(4, 4, 2, 8, RANK)
        return carry

    lax.fori_loop(0, 8, third_mode, 0)
    out.send(pc.at[pl.ds(2 * (1 - core), 2)], rc0, r_c.at[0], sibling)
    scale, factors = start_chain(gram_a, gram_b2)
    recv(rc0, r_c.at[0]).wait_recv()
    pc[pl.ds(2 * core, 2)] += rc0[...]
    for d in (1, 2, 3):
        out.send(
            pc.at[pl.ds(2 * core, 2), lax.rem(x + d, 4)], rc1.at[d - 1], r_c.at[d], at_x(d)
        )
    for q in (0, 1):
        chain_step(q, factors[q], False)
    own_b = b2blk[pl.ds(pl.multiple_of((ia * 2 + ka // 2) * 8, 8), 8), :]
    for s in range(2):
        @pl.when(lax.rem(ka, 2) == s)
        def _():
            b_out[0, 0] = own_b[4 * s:4 * s + 4]

    for d in (1, 2, 3):
        recv(rc1.at[d - 1], r_c.at[d]).wait_recv()
    sc[...] = pc[pl.ds(2 * core, 2), x] + rc1[0] + rc1[1] + rc1[2]
    for d in range(1, 8):
        pz = lax.rem(z + d, 8)
        out.send(
            sc.at[lax.rem(pz // 2, 2), lax.rem(pz, 2)], rc2.at[d - 1], r_c.at[3 + d], at_z(d),
            pz // 4 == core,
        )
    chain_step(2, factors[2], False)

    @pl.when(core == half)
    def _():
        for d in range(1, 8):
            recv(rc2.at[d - 1], r_c.at[3 + d]).wait_recv()
        total = sc[lax.rem(ia, 2), zlo]
        for d in range(7):
            total = total + rc2[d]
        tc[...] = total

    out.send(tc, rc3, r_c.at[11], sibling, core == half)
    chain_step(3, factors[3], False)

    @pl.when(core != half)
    def _():
        recv(rc3, r_c.at[11]).wait_recv()
        tc[...] = rc3[...]

    join(4, tc[...], scale, factors)
    for q in range(4, STEPS - 1):
        chain_step(q, factors[q], True)
    raw = last_step(factors)

    sq1[...] = raw * raw
    for d in (1, 2, 3):
        out.send(sq1, rq1.at[d - 1], r_q.at[d - 1], at_x(d))
    for d in (1, 2, 3):
        recv(rq1.at[d - 1], r_q.at[d - 1]).wait_recv()
    sq2[...] = sq1[...] + rq1[0] + rq1[1] + rq1[2]
    for d in (1, 2, 3):
        out.send(sq2, rq2.at[d - 1], r_q.at[2 + d], at_y(d))
    for d in (1, 2, 3):
        recv(rq2.at[d - 1], r_q.at[2 + d]).wait_recv()
    sq3[...] = sq2[...] + rq2[0] + rq2[1] + rq2[2]
    for d in range(1, 8):
        out.send(sq3, rq3.at[d - 1], r_q.at[5 + d], at_z(d))
    for d in range(1, 8):
        recv(rq3.at[d - 1], r_q.at[5 + d]).wait_recv()
    total = sq3[...]
    for d in range(7):
        total = total + rq3[d]
    spread = jnp.sqrt(jnp.sum(total, axis=0, keepdims=True) / 1024 + EPS)
    final = raw / spread
    for s in range(2):
        @pl.when(core == s)
        def _():
            c_out[0, 0] = final[4 * s:4 * s + 4]

    out.finish()


def hand_over(a_ref, b_ref, c_ref, a_out, b_out, c_out):
    a_out[...] = a_ref[...]
    b_out[...] = b_ref[...]
    c_out[...] = c_ref[...]


def shards(tensor, factor_b, factor_c):
    vmem = pltpu.VMEM
    dma = pltpu.SemaphoreType.DMA
    scratch = [
        vmem((128, 64, 256), BF16),
        vmem((8, 256, 1024), BF16),
        vmem((128, 64, RANK), BF16),
        vmem((128, 16, RANK), BF16),
        vmem((8, RANK), F32),
        vmem((8, RANK), F32),
        vmem((2, 4, 4, 4, 8, RANK), F32),
        vmem((2, 4, 4, 4, 8, RANK), F32),
        vmem((2, 4, 4, 2, 8, RANK), F32),
        vmem((2, 4, 4, 4, 8, RANK), F32),
        vmem((16, 8, RANK), F32),
        vmem((4, 2, 8, RANK), F32),
        vmem((4, 4, 2, 8, RANK), F32),
        vmem((16, 8, RANK), F32),
        vmem((2, 4, 8, RANK), F32),
        vmem((3, 4, 8, RANK), F32),
        vmem((3, 8, RANK), F32),
        vmem((3, 2, 8, RANK), F32),
        vmem((2, 8, RANK), F32),
        vmem((3, 8, RANK), F32),
        vmem((2, 4, 2, 8, RANK), F32),
        vmem((3, 2, 2, 8, RANK), F32),
        vmem((2, 2, 8, RANK), F32),
        vmem((7, 8, RANK), F32),
        vmem((8, RANK), F32),
        vmem((8, RANK), F32),
        vmem((3, 8, RANK), F32),
        vmem((3, 8, RANK), F32),
        vmem((7, 8, RANK), F32),
        vmem((8, RANK), F32),
        vmem((8, RANK), F32),
        vmem((8, RANK), F32),
        vmem((256, RANK), BF16),
        vmem((256, RANK), BF16),
        vmem((RANK, RANK), F32),
        vmem((RANK, RANK), F32),
        vmem((RANK, RANK), F32),
        vmem((RANK, RANK), F32),
        vmem((RANK, RANK), F32),
        vmem((STEPS, RANK + 16, RANK), BF16),
        vmem((STEPS, RANK, RANK), BF16),
        vmem((RANK, RANK), BF16),
        vmem((8, RANK), F32),
        vmem((64, RANK), F32),
        vmem((256, RANK), F32),
        vmem((128, RANK), F32),
        vmem((64, RANK), F32),
        vmem((8, RANK), F32),
        dma((144,)),
        dma((1,)),
        dma((4, 4)),
        dma((4, 4)),
        dma((4, 6)),
        dma((4, 4)),
        dma((9,)),
        dma((6,)),
        dma((12,)),
        dma((13,)),
        dma,
    ]
    results = pl.pallas_call(
        kernel,
        out_shape=(
            jax.ShapeDtypeStruct((1, 1, 2, RANK), F32),
            jax.ShapeDtypeStruct((1, 1, 4, RANK), F32),
            jax.ShapeDtypeStruct((1, 1, 4, RANK), F32),
        ),
        in_specs=[
            pl.BlockSpec(memory_space=pl.ANY),
            pl.BlockSpec(memory_space=pltpu.VMEM),
            pl.BlockSpec(memory_space=pltpu.VMEM),
        ],
        out_specs=[pl.BlockSpec(memory_space=pltpu.VMEM)] * 3,
        scratch_shapes=scratch,
        compiler_params=pltpu.CompilerParams(
            collective_id=0, has_side_effects=True, vmem_limit_bytes=58 * 1024 * 1024
        ),
        name="sweep",
    )(tensor, factor_b, factor_c)
    return pl.pallas_call(
        hand_over,
        out_shape=tuple(jax.ShapeDtypeStruct(r.shape, F32) for r in results),
        name="hand_over",
    )(*results)


def solution(mesh):
    in_specs = (
        P("ia", "ja", "ka"),
        P("ja", ("ia", "ka"), None, None),
        P("ka", ("ia", "ja"), None, None),
    )
    out_specs = (
        P("ia", ("ja", "ka"), None, None),
        P("ja", ("ia", "ka"), None, None),
        P("ka", ("ia", "ja"), None, None),
    )
    return jax.shard_map(shards, mesh=mesh, in_specs=in_specs, out_specs=out_specs, check_vma=False)
```

time: 175 us -> 156 us (0.89)
  Pallas kernels: 171 us -> 155 us
  local copies, waits for them, and re-layouts: 3.86 us -> 0 us
    pallas_call x1, Pallas kernels: 171 us -> 153 us  [shards(): pl.pallas_call(kernel, out_shape=(jax.ShapeDtypeStruct((1, 1, 2, RANK), F...]
    unnamed x3 -> x0, local copies, waits for them, and re-layouts: 3.86 us -> none
where the time goes in v2:
time: 156 us; the launch traced here: 155 us
  Pallas kernels  155 us (99%)
    pallas_call x1, Pallas kernels, shards(): pl.pallas_call(kernel, out_shape=(jax.ShapeDtypeStruct((1, 1, 2, RANK), F...  153 us

profile of v2, /device:TPU:1, one launch (start us, length us, event | category | flops | bytes accessed | tf_op | source)
XLA Modules:
  0.0 155.5 jit_solution(18353122662038339114)
XLA Ops:
  0.6 153.5 %sweep.1 = (f32[1,1,2,512]{3,2,1,0:T(2,128)}, f32[1,1,4,512]{3,2,1,0:T(4,128)}, f32[1,1,4,512]{3,2,1,0:T(4,128)}) custom-call(bf16[128,64,256]{2,1,0:T(8,128)(2,1)} %t_hbm.1, f32[1,1,4,512]{3,2,1,0:T(4,128)} %fb_ref.1, f32[1,1,4,512]{3,2,1,0:T(4,128)} %fc_ref.1), custom_call_target="tpu_custom_call" | custom-call | tf_op jit(solution)/shard_map/sweep/pallas_call | solution.py:766
  154.1 1.3 hand_over.1
